TPU v7x, 32 devices: a whole 2x2x4 slice. The times are simulated.
32 devices in a mesh: shot: 4 (over x, core), brick: 8 (over z, y).
Axes of the slice: x: 2, y: 2, z: 4, core: 2. Of those that a mesh axis runs over, the one named last changes fastest.
Arguments:
- field_prev: float32 [4, 32, 256, 256], P('shot', 'brick'), may hold values from -6 to 6
- field_now: float32 [4, 32, 256, 256], P('shot', 'brick'), may hold values from -6 to 6
- diag_coef: float32 [3, 32, 256, 256], P(None, 'brick'), may hold values from 0.06 to 0.22
- cross_coef: float32 [3, 32, 256, 256], P(None, 'brick'), may hold values from -0.08 to 0.08
- green: bfloat16 [4, 1024, 1024], P('shot', None, 'brick'), may hold values from -0.1875 to 0.1875
- delays: int32 [4], replicated, may hold values from 0 to 8
- past: bfloat16 [8, 4, 1024], P(None, 'shot', 'brick'), may hold values from -6 to 6
- rec_cell: int32 [4, 1024], P('shot', 'brick'), may hold values from 0 to 262143
- emit_cell: int32 [4, 1024], P('shot', 'brick'), may hold values from 0 to 262143
Outputs:
- field_before: float32 [4, 32, 256, 256], P('shot', 'brick')
- field_after: float32 [4, 32, 256, 256], P('shot', 'brick')
- recorded: bfloat16 [3, 4, 1024], P(None, 'shot', 'brick')
Inputs may be any that keep to these rules, and one draw needn't show every extreme that they name: `rec_cell`: entries of block b (points b * 128 to (b + 1) * 128 - 1) index cells of brick b, counted within the brick. `emit_cell`: entries of block b (points b * 128 to (b + 1) * 128 - 1) index cells of brick b, counted within the brick.
All inputs are finite; a program needn't handle non-finite values.
Results may differ from a plain program's by a relative error of at most 0.001.
Values may be sent and summed in bfloat16 or wider, within the bound.
A program may use at most 64 MiB of HBM per device.

v0:
```python
import jax
import jax.numpy as jnp
from jax import lax
from jax.sharding import PartitionSpec as P

STEPS = 3


def with_halo(array, sides, width):
    for axis, dim in sides:
        size, length = (lax.axis_size(axis), array.shape[dim])
        up = [(i, (i + 1) % size) for i in range(size - 1)]
        down = [(j, i) for i, j in up]
        last = lax.slice_in_dim(array, length - width, length, axis=dim)
        leading = lax.slice_in_dim(array, 0, width, axis=dim)
        before = lax.ppermute(last, axis, up)
        after = lax.ppermute(leading, axis, down)
        array = jnp.concatenate([before, array, after], axis=dim)
    return array


def operate(padded, centre, diag_coef, cross_coef):
    width_x = centre.shape[1]
    width_y = centre.shape[2]
    width_z = centre.shape[3]

    def shifted(offset_x, offset_y, offset_z):
        return padded[
            :,
            1 + offset_x : 1 + offset_x + width_x,
            1 + offset_y : 1 + offset_y + width_y,
            1 + offset_z : 1 + offset_z + width_z,
        ]

    second = diag_coef[0] * (shifted(1, 0, 0) - 2.0 * centre + shifted(-1, 0, 0))
    second = second + diag_coef[1] * (shifted(0, 1, 0) - 2.0 * centre + shifted(0, -1, 0))
    second = second + diag_coef[2] * (shifted(0, 0, 1) - 2.0 * centre + shifted(0, 0, -1))
    mixed = cross_coef[0] * (
        shifted(1, 1, 0) - shifted(1, -1, 0) - shifted(-1, 1, 0) + shifted(-1, -1, 0)
    )
    mixed = mixed + cross_coef[1] * (
        shifted(1, 0, 1) - shifted(1, 0, -1) - shifted(-1, 0, 1) + shifted(-1, 0, -1)
    )
    mixed = mixed + cross_coef[2] * (
        shifted(0, 1, 1) - shifted(0, 1, -1) - shifted(0, -1, 1) + shifted(0, -1, -1)
    )
    return second + 0.5 * mixed


def on_device(
    field_prev, field_now, diag_coef, cross_coef, green, delays, past, rec_cell, emit_cell
):
    lag_rank = lax.axis_index("shot")
    steps_total = STEPS
    history = past.shape[0]
    my_delay = lax.dynamic_index_in_dim(delays, lag_rank, 0, keepdims=False)
    series = [lax.all_gather(past, "shot", axis=1, tiled=True)]
    earlier, current = (field_prev, field_now)
    recorded = []
    for moment in range(steps_total):
        flat_now = current.reshape(1, -1)
        sample = jnp.take(flat_now[0], rec_cell[0]).astype(jnp.bfloat16).reshape(1, -1)
        recorded.append(sample)
        series.append(lax.all_gather(sample, "shot", axis=0, tiled=True)[None])
        stacked = jnp.concatenate(series, 0)
        where_at = history + moment - my_delay
        chosen = lax.dynamic_index_in_dim(stacked, where_at, 0, keepdims=False)
        partial_value = lax.dot_general(
            chosen, green[0], (((1,), (1,)), ((), ())), preferred_element_type=jnp.float32
        )
        emitted = lax.psum_scatter(
            partial_value.reshape(-1), ("shot", "brick"), scatter_dimension=0, tiled=True
        )
        extended = with_halo(current, (("brick", 1),), 1)
        padded = jnp.pad(extended, ((0, 0), (0, 0), (1, 1), (1, 1)))
        following = 2.0 * current - earlier + operate(padded, current, diag_coef, cross_coef)
        flat_next = following.reshape(1, -1)
        flat_next = flat_next.at[0, emit_cell[0]].add(emitted)
        earlier, current = (current, flat_next.reshape(current.shape))
    return (earlier, current, jnp.stack(recorded))


def solution(mesh):
    return jax.shard_map(
        on_device,
        mesh=mesh,
        in_specs=(
            P("shot", "brick", None, None),
            P("shot", "brick", None, None),
            P(None, "brick", None, None),
            P(None, "brick", None, None),
            P("shot", None, "brick"),
            P(),
            P(None, "shot", "brick"),
            P("shot", "brick"),
            P("shot", "brick"),
        ),
        out_specs=(
            P("shot", "brick", None, None),
            P("shot", "brick", None, None),
            P(None, "shot", "brick"),
        ),
        check_vma=False,
    )
```

profile of v0, /device:TPU:0, one launch (start us, length us, event | category | flops | bytes accessed | tf_op | source)
XLA Modules:
  0.0 225.1 jit_solution(12524137254115153923)
XLA Ops:
  0.6 0.0 copy-start
  0.6 0.0 copy-start.5
  0.7 0.0 copy-start.6
  0.7 1.9 fusion.69
  2.5 5.6 %collective-permute-start.1 = (f32[1,1,256,256]{3,2,1,0:T(8,128)}, f32[1,1,256,256]{3,2,1,0:T(8,128)}, u32[]{:S(2)}, u32[]{:S(2)}) collective-permute-start(f32[1,1,256,256]{3,2,1,0:T(8,128)} %get-tuple-element.19), channel_id=1, source_target_pairs={{0,1},{1,2},{2,3},{3,4},{4,5},{5,6},{6,7},{8,9},{9,10},{10,11},{11... | collective-permute-start | bytes 786440 | tf_op jit(solution)/shard_map/ppermute | solution.py:16
  8.1 1.3 collective-permute-start
  9.4 1.2 dynamic_slice.16
  12.0 0.7 compare_select_fusion
  12.6 5.3 %all_gather.12 = bf16[8,4,128]{2,0,1:T(8,128)(2,1)S(1)} all-gather(bf16[8,1,128]{2,0,1:T(8,128)(2,1)} %param.17), channel_id=1, replica_groups=mesh['shot'=4,'brick'=8] {'shot'}, dimensions={1}, use_global_device_ids=true | all-gather | bytes 10240 | tf_op jit(solution)/shard_map/all_gather | solution.py:57
  17.9 2.6 %copy.37 = bf16[128,2,8,128]{3,1,2,0:T(2,128)(2,1)} copy(f32[128,2,8,128]{3,2,1,0:T(8,128)} %bitcast.66) | data formatting | bytes 1572864
  20.5 0.0 copy-start.1
  20.5 2.4 %gather_fusion = bf16[128]{0:T(256)(128)(2,1)S(1)} fusion(bf16[262144]{0:T(1024)(128)(2,1)} %bitcast.73, s32[1024]{0:T(1024)S(1)} %pad_clamp_fusion), kind=kCustom, calls=%fused_computation.clone | custom fusion | bytes 1024 | tf_op jit(solution)/shard_map/jit(_take)/gather | solution.py:62
  22.8 0.0 copy-done.5
  22.9 5.0 %all-gather.3 = bf16[4,1,128]{2,1,0:T(2,128)(2,1)S(1)} all-gather(bf16[1,1,128]{2,1,0:T(2,128)(2,1)S(1)} %get-tuple-element.13), channel_id=2, replica_groups=mesh['shot'=4,'brick'=8] {'shot'}, dimensions={0}, use_global_device_ids=true | all-gather | bytes 1280 | tf_op jit(solution)/shard_map/all_gather | solution.py:64
  27.9 0.0 copy-done
  27.9 0.2 convolution_bitcast_fusion.2
  30.7 41.2 %all-reduce.4 = f32[4096]{0:T(1024)S(1)} all-reduce(f32[4096]{0:T(1024)S(1)} %bitcast.74), channel_id=5, replica_groups=mesh['shot'=4,'brick'=8] {'shot','brick'}, use_global_device_ids=true, to_apply=%region_0.2.clone | all-reduce | flops 4096 | bytes 32768
  71.9 0.0 copy-start.4
  71.9 0.1 dynamic-slice
  72.0 0.0 copy-done.6
  72.0 0.0 collective-permute-done.1
  72.0 0.0 collective-permute-done
  72.0 2.2 select_maximum_fusion.4
  74.2 0.0 copy-done.1
  74.2 0.0 copy-done.4
  74.2 5.2 %fusion.37 = f32[1,4,256,256]{3,2,1,0:T(8,128)S(1)} fusion(f32[1,6,258,258]{3,2,1,0:T(8,128)S(1)} %select_maximum_fusion.4, f32[1,4,256,256]{3,2,1,0:T(8,128)S(1)} %copy-done.4, f32[1,1,256,256]{3,2,1,0:T(8,128)} %collective-permute-done.1, f32[1,1,256,256]{3,2,1,0:T(8,128)} %collective-permute-done, f32[1,4,256,256]{3,2,1,0:T(8,128)} %param.11, ...), kind=kLoop, calls=%fused_computation.89 | loop fusion | flops 8388608 | bytes 26738688 | tf_op jit(solution)/shard_map/add | solution.py:76
  79.4 1.5 copy.36
  80.9 3.4 %scatter_fusion = f32[262144]{0:T(1024)} fusion(f32[262144]{0:T(1024)} %bitcast.67, s32[128]{0:T(128)S(1)} %fusion.63, f32[128]{0:T(128)S(1)} %dynamic-slice), kind=kCustom, calls=%fused_computation.3 | custom fusion | flops 128 | bytes 2048 | tf_op jit(solution)/shard_map/scatter-add | solution.py:78
  84.3 2.1 gather_fusion.1
  86.4 2.5 %reshape.130 = f32[1,4,256,256]{3,2,1,0:T(8,128)} reshape(f32[262144]{0:T(1024)} %scatter_fusion) | data formatting | bytes 2097152 | tf_op jit(solution)/shard_map/reshape | solution.py:79
  88.9 1.9 fusion.68
  90.8 4.9 %collective-permute-start.3 = (f32[1,1,256,256]{3,2,1,0:T(8,128)}, f32[1,1,256,256]{3,2,1,0:T(8,128)}, u32[]{:S(2)}, u32[]{:S(2)}) collective-permute-start(f32[1,1,256,256]{3,2,1,0:T(8,128)} %get-tuple-element.17), channel_id=1, source_target_pairs={{0,1},{1,2},{2,3},{3,4},{4,5},{5,6},{6,7},{8,9},{9,10},{10,11},{11... | collective-permute-start | bytes 786440 | tf_op jit(solution)/shard_map/ppermute | solution.py:16
  95.7 1.3 collective-permute-start.2
  97.0 5.0 %all-gather.4 = bf16[4,1,128]{2,1,0:T(2,128)(2,1)S(1)} all-gather(bf16[1,1,128]{2,1,0:T(2,128)(2,1)S(1)} %fusion.65), channel_id=3, replica_groups=mesh['shot'=4,'brick'=8] {'shot'}, dimensions={0}, use_global_device_ids=true | all-gather | bytes 1280 | tf_op jit(solution)/shard_map/all_gather | solution.py:64
  102.1 0.2 convolution_bitcast_fusion.1
  102.3 41.1 %all-reduce.5 = f32[4096]{0:T(1024)S(1)} all-reduce(f32[4096]{0:T(1024)S(1)} %bitcast.75), channel_id=6, replica_groups=mesh['shot'=4,'brick'=8] {'shot','brick'}, use_global_device_ids=true, to_apply=%region_2.4.clone | all-reduce | flops 4096 | bytes 32768
  143.4 0.0 copy-start.2
  143.4 0.1 dynamic-slice.1
  143.5 0.0 collective-permute-done.3
  143.5 0.0 collective-permute-done.2
  143.5 2.2 select_maximum_fusion.2
  145.7 0.0 copy-done.2
  145.7 5.1 %fusion.22 = f32[1,4,256,256]{3,2,1,0:T(8,128)S(1)} fusion(f32[1,6,258,258]{3,2,1,0:T(8,128)S(1)} %select_maximum_fusion.2, f32[1,4,256,256]{3,2,1,0:T(8,128)} %reshape.130, f32[1,1,256,256]{3,2,1,0:T(8,128)} %collective-permute-done.3, f32[1,1,256,256]{3,2,1,0:T(8,128)} %collective-permute-done.2, f32[1,4,256,256]{3,2,1,0:T(8,128)} %param.12, ...), kind=kLoop, calls=%fused_computation.58 | loop fusion | flops 8388608 | bytes 26738688 | tf_op jit(solution)/shard_map/add | solution.py:76
  150.8 1.5 copy.39
  152.3 3.4 %scatter_fusion.1 = f32[262144]{0:T(1024)} fusion(f32[262144]{0:T(1024)} %bitcast.68, s32[128]{0:T(128)S(1)} %fusion.63, f32[128]{0:T(128)S(1)} %dynamic-slice.1), kind=kCustom, calls=%fused_computation.4 | custom fusion | flops 128 | bytes 2048 | tf_op jit(solution)/shard_map/scatter-add | solution.py:78
  155.8 2.1 gather_fusion.2
  157.9 2.5 %reshape.134 = f32[1,4,256,256]{3,2,1,0:T(8,128)} reshape(f32[262144]{0:T(1024)} %scatter_fusion.1) | data formatting | bytes 2097152 | tf_op jit(solution)/shard_map/reshape | solution.py:79
  160.3 1.9 fusion.67
  162.2 4.9 %collective-permute-start.5 = (f32[1,1,256,256]{3,2,1,0:T(8,128)}, f32[1,1,256,256]{3,2,1,0:T(8,128)}, u32[]{:S(2)}, u32[]{:S(2)}) collective-permute-start(f32[1,1,256,256]{3,2,1,0:T(8,128)} %get-tuple-element.15), channel_id=1, source_target_pairs={{0,1},{1,2},{2,3},{3,4},{4,5},{5,6},{6,7},{8,9},{9,10},{10,11},{11... | collective-permute-start | bytes 786440 | tf_op jit(solution)/shard_map/ppermute | solution.py:16
  167.1 1.3 collective-permute-start.4
  168.4 0.6 copy.32
  169.0 5.0 %all-gather.5 = bf16[4,1,128]{2,1,0:T(2,128)(2,1)S(1)} all-gather(bf16[1,1,128]{2,1,0:T(2,128)(2,1)S(1)} %fusion.64), channel_id=4, replica_groups=mesh['shot'=4,'brick'=8] {'shot'}, dimensions={0}, use_global_device_ids=true | all-gather | bytes 1280 | tf_op jit(solution)/shard_map/all_gather | solution.py:64
  174.0 0.2 convolution_bitcast_fusion
  174.2 40.0 %all-reduce.6 = f32[4096]{0:T(1024)S(1)} all-reduce(f32[4096]{0:T(1024)S(1)} %bitcast.76), channel_id=7, replica_groups=mesh['shot'=4,'brick'=8] {'shot','brick'}, use_global_device_ids=true, to_apply=%region_4.6.clone | all-reduce | flops 4096 | bytes 32768
  214.2 0.0 copy-start.3
  214.2 0.1 dynamic-slice.2
  214.3 0.0 collective-permute-done.5
  214.3 0.0 collective-permute-done.4
  214.3 2.2 select_maximum_fusion
  216.5 0.0 copy-done.3
  216.5 5.1 %fusion.7 = f32[1,4,256,256]{3,2,1,0:T(8,128)S(1)} fusion(f32[1,6,258,258]{3,2,1,0:T(8,128)S(1)} %select_maximum_fusion, f32[1,4,256,256]{3,2,1,0:T(8,128)} %reshape.134, f32[1,1,256,256]{3,2,1,0:T(8,128)} %collective-permute-done.5, f32[1,1,256,256]{3,2,1,0:T(8,128)} %collective-permute-done.4, f32[1,4,256,256]{3,2,1,0:T(8,128)} %reshape.130, ...), kind=kLoop, calls=%fused_computation.27 | loop fusion | flops 8388608 | bytes 26738688 | tf_op jit(solution)/shard_map/add | solution.py:76
  221.6 0.5 copy.41
  222.2 1.7 scatter_fusion.2
  223.8 1.3 reshape.138
  (12 shorter events, 0.1 us)
Async XLA Ops:
  0.6 27.3 %copy-start = (bf16[1,1024,128]{2,1,0:T(8,128)(2,1)S(1)}, bf16[1,1024,128]{2,1,0:T(8,128)(2,1)}, u32[]{:S(2)}) copy-start(bf16[1,1024,128]{2,1,0:T(8,128)(2,1)} %param.15) | copy-start | bytes 786436
  0.6 22.2 %copy-start.5 = (s32[1,128]{1,0:T(1,128)S(1)}, s32[1,128]{1,0:T(1,128)}, u32[]{:S(2)}) copy-start(s32[1,128]{1,0:T(1,128)} %param.18) | copy-start | bytes 1540
  0.7 71.3 %copy-start.6 = (s32[1,128]{1,0:T(1,128)S(1)}, s32[1,128]{1,0:T(1,128)}, u32[]{:S(2)}) copy-start(s32[1,128]{1,0:T(1,128)} %param.19) | copy-start | bytes 1540
  2.5 69.4 %collective-permute-start.1 = (f32[1,1,256,256]{3,2,1,0:T(8,128)}, f32[1,1,256,256]{3,2,1,0:T(8,128)}, u32[]{:S(2)}, u32[]{:S(2)}) collective-permute-start(f32[1,1,256,256]{3,2,1,0:T(8,128)} %get-tuple-element.19), channel_id=1, source_target_pairs={{0,1},{1,2},{2,3},{3,4},{4,5},{5,6},{6,7},{8,9},{9,10},{10,11},{11... | collective-permute-start | bytes 786440 | tf_op jit(solution)/shard_map/ppermute | solution.py:16
  8.1 63.9 %collective-permute-start = (f32[1,1,256,256]{3,2,1,0:T(8,128)}, f32[1,1,256,256]{3,2,1,0:T(8,128)}, u32[]{:S(2)}, u32[]{:S(2)}) collective-permute-start(f32[1,1,256,256]{3,2,1,0:T(8,128)} %get-tuple-element.20), channel_id=1, source_target_pairs={{1,0},{2,1},{3,2},{4,3},{5,4},{6,5},{7,6},{9,8},{10,9},{11,10},{12... | collective-permute-start | bytes 786440 | tf_op jit(solution)/shard_map/ppermute | solution.py:17
  20.5 53.7 %copy-start.1 = (f32[3,4,256,256]{3,2,1,0:T(8,128)S(1)}, f32[3,4,256,256]{3,2,1,0:T(8,128)}, u32[]{:S(2)}) copy-start(f32[3,4,256,256]{3,2,1,0:T(8,128)} %param.14) | copy-start | bytes 9437188
  71.9 2.3 %copy-start.4 = (f32[1,4,256,256]{3,2,1,0:T(8,128)S(1)}, f32[1,4,256,256]{3,2,1,0:T(8,128)}, u32[]{:S(2)}) copy-start(f32[1,4,256,256]{3,2,1,0:T(8,128)} %param.12) | copy-start | bytes 3145732
  90.8 52.7 %collective-permute-start.3 = (f32[1,1,256,256]{3,2,1,0:T(8,128)}, f32[1,1,256,256]{3,2,1,0:T(8,128)}, u32[]{:S(2)}, u32[]{:S(2)}) collective-permute-start(f32[1,1,256,256]{3,2,1,0:T(8,128)} %get-tuple-element.17), channel_id=1, source_target_pairs={{0,1},{1,2},{2,3},{3,4},{4,5},{5,6},{6,7},{8,9},{9,10},{10,11},{11... | collective-permute-start | bytes 786440 | tf_op jit(solution)/shard_map/ppermute | solution.py:16
  95.7 47.7 %collective-permute-start.2 = (f32[1,1,256,256]{3,2,1,0:T(8,128)}, f32[1,1,256,256]{3,2,1,0:T(8,128)}, u32[]{:S(2)}, u32[]{:S(2)}) collective-permute-start(f32[1,1,256,256]{3,2,1,0:T(8,128)} %get-tuple-element.18), channel_id=1, source_target_pairs={{1,0},{2,1},{3,2},{4,3},{5,4},{6,5},{7,6},{9,8},{10,9},{11,10},{12... | collective-permute-start | bytes 786440 | tf_op jit(solution)/shard_map/ppermute | solution.py:17
  143.4 2.4 %copy-start.2 = (f32[3,4,256,256]{3,2,1,0:T(8,128)S(1)}, f32[3,4,256,256]{3,2,1,0:T(8,128)}, u32[]{:S(2)}) copy-start(f32[3,4,256,256]{3,2,1,0:T(8,128)} %param.13) | copy-start | bytes 9437188
  162.2 52.1 %collective-permute-start.5 = (f32[1,1,256,256]{3,2,1,0:T(8,128)}, f32[1,1,256,256]{3,2,1,0:T(8,128)}, u32[]{:S(2)}, u32[]{:S(2)}) collective-permute-start(f32[1,1,256,256]{3,2,1,0:T(8,128)} %get-tuple-element.15), channel_id=1, source_target_pairs={{0,1},{1,2},{2,3},{3,4},{4,5},{5,6},{6,7},{8,9},{9,10},{10,11},{11... | collective-permute-start | bytes 786440 | tf_op jit(solution)/shard_map/ppermute | solution.py:16
  167.1 47.1 %collective-permute-start.4 = (f32[1,1,256,256]{3,2,1,0:T(8,128)}, f32[1,1,256,256]{3,2,1,0:T(8,128)}, u32[]{:S(2)}, u32[]{:S(2)}) collective-permute-start(f32[1,1,256,256]{3,2,1,0:T(8,128)} %get-tuple-element.16), channel_id=1, source_target_pairs={{1,0},{2,1},{3,2},{4,3},{5,4},{6,5},{7,6},{9,8},{10,9},{11,10},{12... | collective-permute-start | bytes 786440 | tf_op jit(solution)/shard_map/ppermute | solution.py:17
  214.2 2.4 %copy-start.3 = (f32[3,4,256,256]{3,2,1,0:T(8,128)S(1)}, f32[3,4,256,256]{3,2,1,0:T(8,128)}, u32[]{:S(2)}) copy-start(f32[3,4,256,256]{3,2,1,0:T(8,128)} %param.13) | copy-start | bytes 9437188
where the time goes:
time: 226 us; the launch traced here: 225 us
  blocking collectives  143 us (63%)
  other arithmetic  31.3 us (14%)
  local copies, waits for them, and re-layouts  26.7 us (12%)
  starting transfers between devices  19.3 us (9%)
  between operations  4.8 us (2%)
    unnamed x3, blocking collectives  122 us
    ppermute x3, starting transfers between devices, with_halo(): before = lax.ppermute(last, axis, up)  15.4 us
    add x3, other arithmetic, on_device(): 2.0 * current - earlier + operate(padded, current, diag_coef, cross_coef)  15.4 us
    all_gather x3, blocking collectives, on_device(): series.append(lax.all_gather(sample, 'shot', axis=0, tiled=True)[None])  15.1 us
    scatter-add x3, other arithmetic, on_device(): flat_next = flat_next.at[0, emit_cell[0]].add(emitted)  8.47 us
    unnamed x25, local copies, waits for them, and re-layouts  7.02 us
    concatenate x3, other arithmetic, with_halo(): array = jnp.concatenate([before, array, after], axis=dim)  6.63 us
    gather x3, local copies, waits for them, and re-layouts, on_device(): jnp.take(flat_now[0], rec_cell[0]).astype(jnp.bfloat16).reshape(1, -1)  6.54 us
  transfers between devices with their start and end apart: 6, of which 0 were waited for; matrix products, arithmetic and copies ran while one was open for 4% of the time, Pallas kernels for 0%

commit v1 on v0

v1 whole, which is shorter than its diff:
```python
import functools

import jax
import jax.numpy as jnp
from jax import lax
from jax.experimental import pallas as pl
from jax.experimental.pallas import tpu as pltpu
from jax.sharding import PartitionSpec as P

STEPS = 3
MESH = pl.DeviceIdType.MESH
PAD = 8
ROWS = 16
CHUNKS = 4
F32 = jnp.float32
BF16 = jnp.bfloat16


def column_of(row):
    k = row.shape[1]
    eye = lax.broadcasted_iota(jnp.int32, (k, k), 0) == lax.broadcasted_iota(jnp.int32, (k, k), 1)
    return jnp.sum(jnp.where(eye, jnp.broadcast_to(row, (k, k)), 0.0), axis=1, keepdims=True)


def row_of(col):
    k = col.shape[0]
    eye = lax.broadcasted_iota(jnp.int32, (k, k), 0) == lax.broadcasted_iota(jnp.int32, (k, k), 1)
    return jnp.sum(jnp.where(eye, jnp.broadcast_to(col, (k, k)), 0.0), axis=0, keepdims=True)


def kernel(
    n, shots, prev_hbm, now_hbm, diag_hbm, cross_hbm, green_hbm, delays, past, rec_cell, emit_cell,
    before_hbm, after_hbm, recorded,
    ua, ub, diag, cross, green, series, send_edge, recv_edge, send_sum, recv_sum,
    rec_rows, rec_lanes, emit_rows, emit_lanes, weights,
    now_sem, prev_sem, coef_sem, green_sem, green_send, green_recv, pass_send, pass_recv,
    edge_send, edge_recv, sum_send, sum_recv, out_sem,
):
    me = lax.axis_index("brick")
    shot = lax.axis_index("shot")
    cx, ny, nz = prev_hbm.shape[1:]
    hist = past.shape[0]
    points = rec_cell.shape[1]
    chunk = ny // CHUNKS
    half = shots // 2
    core = lax.rem(shot, 2)
    high = shot // 2
    peer = shot + 1 - 2 * core
    inner = pl.ds(PAD, ny)

    order = [0, cx - 1] + list(range(1, cx - 1))

    def now_copy(x):
        return pltpu.make_async_copy(now_hbm.at[0, x], ub.at[1 + x, inner], now_sem.at[x])

    def prev_copy(x):
        return pltpu.make_async_copy(prev_hbm.at[0, x], ua.at[1 + x, inner], prev_sem.at[x])

    def diag_copy(x):
        return pltpu.make_async_copy(diag_hbm.at[:, x], diag.at[:, x], coef_sem.at[0, x])

    def cross_copy(x):
        return pltpu.make_async_copy(cross_hbm.at[:, x], cross.at[:, x], coef_sem.at[1, x])

    for x in order:
        now_copy(x).start()

    barrier = pltpu.get_barrier_semaphore()
    for i in range(1, n):
        pl.semaphore_signal(
            barrier, inc=1, device_id=(shot, lax.rem(me + i, n)), device_id_type=MESH
        )
    for i in range(1, half):
        pl.semaphore_signal(
            barrier, inc=1, device_id=(lax.rem(high + i, half) * 2 + core, me), device_id_type=MESH
        )
    pl.semaphore_signal(barrier, inc=1, device_id=(peer, me), device_id_type=MESH)

    own_green = pltpu.make_async_copy(green_hbm.at[0], green.at[shot], green_sem)
    own_green.start()
    for x in order[2:] + order[:2]:
        prev_copy(x).start()
        diag_copy(x).start()
        cross_copy(x).start()

    for field in (ua, ub):
        field[0] = jnp.zeros(field.shape[1:], F32)
        field[cx + 1] = jnp.zeros(field.shape[1:], F32)
        for x in range(cx):
            field[1 + x, pl.ds(0, PAD)] = jnp.zeros((PAD, nz), F32)
            field[1 + x, pl.ds(PAD + ny, PAD)] = jnp.zeros((PAD, nz), F32)

    pl.semaphore_wait(barrier, n - 1 + half)

    def green_copy(i):
        return pltpu.make_async_remote_copy(
            src_ref=green_hbm.at[0],
            dst_ref=green.at[shot],
            send_sem=green_send.at[i],
            recv_sem=green_recv.at[i],
            device_id=(lax.rem(high + i, half) * 2 + core, me) if i else (peer, me),
            device_id_type=MESH,
        )

    def green_wait(i):
        source = lax.rem(high - i + half, half) * 2 + core if i else peer
        pltpu.make_async_remote_copy(
            src_ref=green_hbm.at[0],
            dst_ref=green.at[source],
            send_sem=green_send.at[i],
            recv_sem=green_recv.at[i],
            device_id=(peer, me),
            device_id_type=MESH,
        ).wait_recv()

    def pass_copy(i, which):
        slot = lax.rem(high - i + half, half) * 2 + which
        return pltpu.make_async_remote_copy(
            src_ref=green.at[slot],
            dst_ref=green.at[slot],
            send_sem=pass_send.at[i],
            recv_sem=pass_recv.at[i],
            device_id=(peer, me),
            device_id_type=MESH,
        )

    for i in list(range(1, half)) + [0]:
        green_copy(i).start()

    def edge_copy(t, side, k):
        rows = pl.ds(k * chunk, chunk)
        return pltpu.make_async_remote_copy(
            src_ref=send_edge.at[t, side, rows],
            dst_ref=recv_edge.at[t, side, rows],
            send_sem=edge_send.at[t, side, k],
            recv_sem=edge_recv.at[t, side, k],
            device_id=(shot, lax.rem(me + 1 - 2 * side + n, n)),
            device_id_type=MESH,
        )

    def sends_to(side):
        return me < n - 1 if side == 0 else me > 0

    def hears_from(side):
        return me > 0 if side == 0 else me < n - 1

    def send_edges(field, t, k):
        for side in (0, 1):
            plane = cx if side == 0 else 1
            send_edge[t, side, pl.ds(k * chunk, chunk)] = field[
                plane, pl.ds(PAD + k * chunk, chunk)
            ].astype(BF16)

            @pl.when(sends_to(side))
            def _():
                edge_copy(t, side, k).start()

    def take_edges(field, t, k):
        for side in (0, 1):
            plane = 0 if side == 0 else cx + 1

            @pl.when(hears_from(side))
            def _():
                edge_copy(t, side, k).wait_recv()
                field[plane, pl.ds(PAD + k * chunk, chunk)] = recv_edge[
                    t, side, pl.ds(k * chunk, chunk)
                ].astype(F32)

    now_copy(0).wait()
    now_copy(cx - 1).wait()
    for k in range(CHUNKS):
        send_edges(ub, 0, k)

    cells = rec_cell[...]
    row_col = column_of((cells // nz).astype(F32))
    lane_col = column_of((cells % nz).astype(F32))
    rec_rows[...] = jnp.where(
        lax.broadcasted_iota(jnp.int32, (points, cx * ny), 1).astype(F32) == row_col, 1.0, 0.0
    ).astype(BF16)
    lanes = lax.broadcasted_iota(jnp.int32, (points, nz), 1).astype(F32)
    rec_lanes[...] = jnp.where(lanes == lane_col, 1.0, 0.0)
    cells = emit_cell[...]
    hits = jnp.where(
        lax.broadcasted_iota(jnp.int32, (cx * ny, points), 0) == cells // nz, 1.0, 0.0
    ).astype(BF16)
    emit_rows[:, pl.ds(0, points)] = hits
    emit_rows[:, pl.ds(points, points)] = hits
    emit_lanes[...] = jnp.where(lanes == column_of((cells % nz).astype(F32)), 1.0, 0.0)
    series[...] = jnp.zeros(series.shape, F32)
    series[pl.ds(0, hist), :] = past[...]

    def record(field, t):
        picked = jnp.zeros((points, nz), F32)
        for x in range(cx):
            picked = picked + jnp.dot(
                rec_rows[:, pl.ds(x * ny, ny)],
                field[1 + x, inner].astype(BF16),
                preferred_element_type=F32,
            )
        sample = row_of(jnp.sum(picked * rec_lanes[...], axis=1, keepdims=True))
        recorded[pl.ds(t, 1), :] = sample
        series[pl.ds(hist + t, 1), :] = sample

    def sum_copy(t, i):
        to = lax.rem(me + i, n)
        return pltpu.make_async_remote_copy(
            src_ref=send_sum.at[t, to],
            dst_ref=recv_sum.at[t, me],
            send_sem=sum_send.at[t, i - 1],
            recv_sem=sum_recv.at[t, i - 1],
            device_id=(shot, to),
            device_id_type=MESH,
        )

    def sum_wait(t, i):
        pltpu.make_async_remote_copy(
            src_ref=send_sum.at[t, lax.rem(me + i, n)],
            dst_ref=recv_sum.at[t, lax.rem(me - i + n, n)],
            send_sem=sum_send.at[t, i - 1],
            recv_sem=sum_recv.at[t, i - 1],
            device_id=(shot, lax.rem(me + i, n)),
            device_id_type=MESH,
        ).wait_recv()

    def emit_start(t):
        total = None
        steps_of = lax.broadcasted_iota(jnp.int32, series.shape, 0)
        for lag in range(shots):
            where_at = hist + t - delays[lag]
            chosen = jnp.sum(jnp.where(steps_of == where_at, series[...], 0.0), axis=0, keepdims=True)
            part = lax.dot_general(
                jnp.broadcast_to(chosen, (16, points)).astype(BF16),
                green[lag],
                (((1,), (1,)), ((), ())),
                preferred_element_type=F32,
            )
            total = part if total is None else total + part
        for k in range(n):
            send_sum[t, k] = total[0:1, k * points:(k + 1) * points]
        for i in range(1, n):
            sum_copy(t, i).start()
        recv_sum[t, me] = send_sum[t, me]

    def emit_finish(t):
        for i in range(1, n):
            sum_wait(t, i)
        total = recv_sum[t, 0]
        for k in range(1, n):
            total = total + recv_sum[t, k]
        spread = emit_lanes[...] * column_of(total)
        upper = spread.astype(BF16)
        weights[pl.ds(0, points), :] = upper
        weights[pl.ds(points, points), :] = (spread - upper.astype(F32)).astype(BF16)

    def add_emission(field, x, start, rows):
        field[1 + x, pl.ds(PAD + start, rows)] += jnp.dot(
            emit_rows[pl.ds(x * ny + start, rows), :], weights[...], preferred_element_type=F32
        )

    lane = lax.broadcasted_iota(jnp.int32, (ROWS, nz), 1)
    not_first = lane > 0
    not_last = lane < nz - 1

    def ahead(v):
        return jnp.where(not_last, pltpu.roll(v, nz - 1, 1), 0.0)

    def behind(v):
        return jnp.where(not_first, pltpu.roll(v, 1, 1), 0.0)

    def later(slab):
        return pltpu.roll(slab, ROWS + 2 * PAD - 1, 0)[PAD:PAD + ROWS]

    def sooner(slab):
        return pltpu.roll(slab, 1, 0)[PAD:PAD + ROWS]

    def advance(earlier, current, x, start, rows):
        def body(i, _):
            y = pl.multiple_of(start + i * ROWS, ROWS)
            here = pl.ds(pl.multiple_of(y + PAD, PAD), ROWS)
            around = pl.ds(y, ROWS + 2 * PAD)
            at = pl.ds(y, ROWS)
            centre = current[1 + x, around]
            difference = current[2 + x, around] - current[x, around]
            u = current[1 + x, here]
            above, below = current[2 + x, here], current[x, here]
            u_up, u_down = later(centre), sooner(centre)
            twice = 2.0 * u
            second = diag[0, x, at] * (above + below - twice)
            second = second + diag[1, x, at] * (u_up + u_down - twice)
            second = second + diag[2, x, at] * (ahead(u) + behind(u) - twice)
            across = above - below
            slope = u_up - u_down
            mixed = cross[0, x, at] * (
                later(difference) - sooner(difference)
            )
            mixed = mixed + cross[1, x, at] * (ahead(across) - behind(across))
            mixed = mixed + cross[2, x, at] * (ahead(slope) - behind(slope))
            earlier[1 + x, here] = twice - earlier[1 + x, here] + second + 0.5 * mixed
            return 0

        lax.fori_loop(0, rows // ROWS, body, 0)

    for x in range(1, cx - 1):
        now_copy(x).wait()

    for t in range(STEPS):
        earlier, current = (ua, ub) if t % 2 == 0 else (ub, ua)
        record(current, t)
        if t > 0:
            emit_start(t)
        for x in range(1, cx - 1):
            if t == 0:
                prev_copy(x).wait()
                diag_copy(x).wait()
                cross_copy(x).wait()
            advance(earlier, current, x, 0, ny)
        if t == 0:
            for i in range(1, half):
                green_wait(i)
                pass_copy(i, core).start()
            own_green.wait()
            green_wait(0)
            for i in range(1, half):
                pass_copy(i, 1 - core).wait_recv()
            emit_start(t)
            for x in (0, cx - 1):
                prev_copy(x).wait()
                diag_copy(x).wait()
                cross_copy(x).wait()
        emit_finish(t)
        for x in range(1, cx - 1):
            add_emission(earlier, x, 0, ny)
        take_edges(current, t, 0)
        for k in range(CHUNKS):
            if k + 1 < CHUNKS:
                take_edges(current, t, k + 1)
            for x in (0, cx - 1):
                advance(earlier, current, x, k * chunk, chunk)
                add_emission(earlier, x, k * chunk, chunk)
            if t + 1 < STEPS:
                send_edges(earlier, t + 1, k)
        if t == STEPS - 2:
            before = pltpu.make_async_copy(
                earlier.at[pl.ds(1, cx), inner], before_hbm.at[0], out_sem.at[0]
            )
            before.start()
        if t == STEPS - 1:
            after = pltpu.make_async_copy(
                earlier.at[pl.ds(1, cx), inner], after_hbm.at[0], out_sem.at[1]
            )
            after.start()

    for i in range(half):
        green_copy(i).wait_send()
    for i in range(1, half):
        pass_copy(i, core).wait_send()
    for t in range(STEPS):
        for i in range(1, n):
            sum_copy(t, i).wait_send()
        for side in (0, 1):

            @pl.when(sends_to(side))
            def _():
                for k in range(CHUNKS):
                    edge_copy(t, side, k).wait_send()

    before.wait()
    after.wait()


def on_device(
    n, shots, field_prev, field_now, diag_coef, cross_coef, green, delays, past, rec_cell, emit_cell
):
    _, cx, ny, nz = field_prev.shape
    hist, _, points = past.shape
    _, emits, _ = green.shape
    half = shots // 2
    vmem = pl.BlockSpec(memory_space=pltpu.VMEM)
    hbm = pl.BlockSpec(memory_space=pl.ANY)
    dma = pltpu.SemaphoreType.DMA
    depth = -(-(hist + STEPS) // 8) * 8
    before, after, recorded = pl.pallas_call(
        functools.partial(kernel, n, shots),
        out_shape=(
            jax.ShapeDtypeStruct(field_prev.shape, F32),
            jax.ShapeDtypeStruct(field_prev.shape, F32),
            jax.ShapeDtypeStruct((STEPS, points), F32),
        ),
        in_specs=[hbm] * 5 + [pl.BlockSpec(memory_space=pltpu.SMEM)] + [vmem] * 3,
        out_specs=(hbm, hbm, vmem),
        scratch_shapes=[
            pltpu.VMEM((cx + 2, ny + 2 * PAD, nz), F32),
            pltpu.VMEM((cx + 2, ny + 2 * PAD, nz), F32),
            pltpu.VMEM((3, cx, ny, nz), F32),
            pltpu.VMEM((3, cx, ny, nz), F32),
            pltpu.VMEM((shots, emits, points), BF16),
            pltpu.VMEM((depth, points), F32),
            pltpu.VMEM((STEPS, 2, ny, nz), BF16),
            pltpu.VMEM((STEPS, 2, ny, nz), BF16),
            pltpu.VMEM((STEPS, n, 1, points), F32),
            pltpu.VMEM((STEPS, n, 1, points), F32),
            pltpu.VMEM((points, cx * ny), BF16),
            pltpu.VMEM((points, nz), F32),
            pltpu.VMEM((cx * ny, 2 * points), BF16),
            pltpu.VMEM((points, nz), F32),
            pltpu.VMEM((2 * points, nz), BF16),
            dma((cx,)),
            dma((cx,)),
            dma((2, cx)),
            dma,
            dma((half,)),
            dma((half,)),
            dma((half,)),
            dma((half,)),
            dma((STEPS, 2, CHUNKS)),
            dma((STEPS, 2, CHUNKS)),
            dma((STEPS, n - 1)),
            dma((STEPS, n - 1)),
            dma((2,)),
        ],
        compiler_params=pltpu.CompilerParams(
            collective_id=0, has_side_effects=True, vmem_limit_bytes=48 * 1024 * 1024
        ),
    )(
        field_prev,
        field_now,
        diag_coef,
        cross_coef,
        green,
        delays,
        past.reshape(hist, points).astype(F32),
        rec_cell,
        emit_cell,
    )
    return before, after, recorded.astype(BF16).reshape(STEPS, 1, points)


def solution(mesh):
    return jax.shard_map(
        functools.partial(on_device, mesh.shape["brick"], mesh.shape["shot"]),
        mesh=mesh,
        in_specs=(
            P("shot", "brick", None, None),
            P("shot", "brick", None, None),
            P(None, "brick", None, None),
            P(None, "brick", None, None),
            P("shot", None, "brick"),
            P(),
            P(None, "shot", "brick"),
            P("shot", "brick"),
            P("shot", "brick"),
        ),
        out_specs=(
            P("shot", "brick", None, None),
            P("shot", "brick", None, None),
            P(None, "shot", "brick"),
        ),
        check_vma=False,
    )
```

time: 226 us -> 53.5 us (0.24)
  blocking collectives: 143 us -> 0 us
  Pallas kernels: 0 us -> 44 us
  other arithmetic: 31.3 us -> 1.25 us
  local copies, waits for them, and re-layouts: 26.7 us -> 7.3 us
  starting transfers between devices: 19.3 us -> 0 us
  between operations: 4.8 us -> 0.65 us
    unnamed x3 -> x0, blocking collectives: 122 us -> none
    pallas_call x0 -> x1, Pallas kernels: none -> 44 us  [on_device(): pl.pallas_call(functools.partial(kernel, n, shots), out_shape=(jax.ShapeD...]
    all_gather x4 -> x0, blocking collectives: 20.4 us -> none  [the longest x3 15.1 us: on_device(): series.append(lax.all_gather(sample, 'shot', axis=0, tiled=True)[None])]
    ppermute x6 -> x0, starting transfers between devices: 19.3 us -> none  [the longest x3 15.4 us: with_halo(): before = lax.ppermute(last, axis, up)]
    add x3 -> x0, other arithmetic: 15.4 us -> none  [on_device(): 2.0 * current - earlier + operate(padded, current, diag_coef, cross_coef)]
    scatter-add x3 -> x0, other arithmetic: 8.47 us -> none  [on_device(): flat_next = flat_next.at[0, emit_cell[0]].add(emitted)]
    concatenate x7 -> x0, other arithmetic: 6.71 us -> none  [the longest x3 6.63 us: with_halo(): array = jnp.concatenate([before, array, after], axis=dim)]
    gather x3 -> x0, local copies, waits for them, and re-layouts: 6.54 us -> none  [on_device(): jnp.take(flat_now[0], rec_cell[0]).astype(jnp.bfloat16).reshape(1, -1)]
  transfers between devices with their start and end apart: 6 -> 0, of which waited for: 0 -> 0; matrix products, arithmetic and copies ran while one was open for 4% -> 0% of each run, Pallas kernels for 0% -> 0%
where the time goes in v1:
time: 53.5 us; the launch traced here: 53.2 us
  Pallas kernels  44 us (82%)
  local copies, waits for them, and re-layouts  7.3 us (14%)
  other arithmetic  1.25 us (2%)
  between operations  0.65 us (1%)
    pallas_call x1, Pallas kernels, on_device(): pl.pallas_call(functools.partial(kernel, n, shots), out_shape=(jax.ShapeD...  44 us
    unnamed x14, local copies, waits for them, and re-layouts  7.3 us

profile of v1, /device:TPU:0, one launch (start us, length us, event | category | flops | bytes accessed | tf_op | source)
XLA Modules:
  0.0 53.2 jit_solution(8153361715061533911)
XLA Ops:
  0.6 0.7 %bitcast_convert_fusion.past = f32[8,128]{1,0:T(8,128)S(1)} fusion(bf16[8,1,128]{2,0,1:T(8,128)(2,1)} %param.15), kind=kLoop, calls=%fused_computation | loop fusion | flops 1024 | bytes 6144 | tf_op jit(solution)/shard_map/convert_element_type | solution.py:431
  1.3 0.0 copy-start
  1.3 1.2 %copy-done = f32[1,4,256,256]{3,2,1,0:T(8,128)S(1)} copy-done((f32[1,4,256,256]{3,2,1,0:T(8,128)S(1)}, f32[1,4,256,256]{3,2,1,0:T(8,128)}, u32[]{:S(2)}) %copy-start) | copy-done | bytes 1048600
  2.5 0.0 copy-start.1
  2.5 1.2 %copy-done.1 = f32[1,4,256,256]{3,2,1,0:T(8,128)S(1)} copy-done((f32[1,4,256,256]{3,2,1,0:T(8,128)S(1)}, f32[1,4,256,256]{3,2,1,0:T(8,128)}, u32[]{:S(2)}) %copy-start.1) | copy-done | bytes 1048600
  3.8 0.0 copy-start.2
  3.8 0.9 %copy-done.2 = bf16[1,1024,128]{2,1,0:T(8,128)(2,1)S(1)} copy-done((bf16[1,1024,128]{2,1,0:T(8,128)(2,1)S(1)}, bf16[1,1024,128]{2,1,0:T(8,128)(2,1)}, u32[]{:S(2)}) %copy-start.2) | copy-done | bytes 262168
  4.7 0.0 copy-start.3
  4.7 0.7 %copy-done.3 = s32[4]{0:T(128)S(1)} copy-done((s32[4]{0:T(128)S(1)}, s32[4]{0:T(128)}, u32[]{:S(2)}) %copy-start.3) | copy-done | bytes 40
  5.4 0.0 copy-start.4
  5.4 0.7 %copy-done.4 = s32[1,128]{1,0:T(1,128)S(1)} copy-done((s32[1,128]{1,0:T(1,128)S(1)}, s32[1,128]{1,0:T(1,128)}, u32[]{:S(2)}) %copy-start.4) | copy-done | bytes 536
  6.0 0.0 copy-start.5
  6.0 0.7 %copy-done.5 = s32[1,128]{1,0:T(1,128)S(1)} copy-done((s32[1,128]{1,0:T(1,128)S(1)}, s32[1,128]{1,0:T(1,128)}, u32[]{:S(2)}) %copy-start.5) | copy-done | bytes 536
  6.7 44.0 %shard_map.112 = (f32[1,4,256,256]{3,2,1,0:T(8,128)S(1)}, f32[1,4,256,256]{3,2,1,0:T(8,128)S(1)}, f32[3,128]{1,0:T(4,128)S(1)}) custom-call(f32[1,4,256,256]{3,2,1,0:T(8,128)S(1)} %copy-done, f32[1,4,256,256]{3,2,1,0:T(8,128)S(1)} %copy-done.1, f32[3,4,256,256]{3,2,1,0:T(8,128)} %diag_hbm.1, f32[3,4,256,256]{3,2,1,0:T(8,128)} %cross_hbm.1, ...), custom_call_target="tpu_custom_call" | custom-call | tf_op jit(solution)/shard_map/pallas_call | solution.py:382
  50.7 0.6 %convert_bitcast_fusion = bf16[3,1,128]{2,0,1:T(4,128)(2,1)} fusion(f32[3,128]{1,0:T(4,128)S(1)} %get-tuple-element.8), kind=kLoop, calls=%fused_computation.1 | loop fusion | flops 384 | bytes 2304 | tf_op jit(solution)/shard_map/reshape | solution.py:435
  51.2 1.0 %copy.14 = f32[1,4,256,256]{3,2,1,0:T(8,128)} copy(f32[1,4,256,256]{3,2,1,0:T(8,128)S(1)} %get-tuple-element.12) | data formatting | bytes 2097152
  52.2 1.0 %copy.15 = f32[1,4,256,256]{3,2,1,0:T(8,128)} copy(f32[1,4,256,256]{3,2,1,0:T(8,128)S(1)} %get-tuple-element.13) | data formatting | bytes 2097152
Async XLA Ops:
  1.3 1.2 %copy-start = (f32[1,4,256,256]{3,2,1,0:T(8,128)S(1)}, f32[1,4,256,256]{3,2,1,0:T(8,128)}, u32[]{:S(2)}) copy-start(f32[1,4,256,256]{3,2,1,0:T(8,128)} %prev_hbm.1) | copy-start | bytes 3145732
  2.5 1.2 %copy-start.1 = (f32[1,4,256,256]{3,2,1,0:T(8,128)S(1)}, f32[1,4,256,256]{3,2,1,0:T(8,128)}, u32[]{:S(2)}) copy-start(f32[1,4,256,256]{3,2,1,0:T(8,128)} %now_hbm.1) | copy-start | bytes 3145732
  3.8 0.9 %copy-start.2 = (bf16[1,1024,128]{2,1,0:T(8,128)(2,1)S(1)}, bf16[1,1024,128]{2,1,0:T(8,128)(2,1)}, u32[]{:S(2)}) copy-start(bf16[1,1024,128]{2,1,0:T(8,128)(2,1)} %green_hbm.1) | copy-start | bytes 786436
  4.7 0.7 %copy-start.3 = (s32[4]{0:T(128)S(1)}, s32[4]{0:T(128)}, u32[]{:S(2)}) copy-start(s32[4]{0:T(128)} %delays.1) | copy-start | bytes 52
  5.4 0.7 %copy-start.4 = (s32[1,128]{1,0:T(1,128)S(1)}, s32[1,128]{1,0:T(1,128)}, u32[]{:S(2)}) copy-start(s32[1,128]{1,0:T(1,128)} %rec_cell.1) | copy-start | bytes 1540
  6.0 0.7 %copy-start.5 = (s32[1,128]{1,0:T(1,128)S(1)}, s32[1,128]{1,0:T(1,128)}, u32[]{:S(2)}) copy-start(s32[1,128]{1,0:T(1,128)} %emit_cell.1) | copy-start | bytes 1540

commit v2 on v1

--- a/solution.py
+++ b/solution.py
@@ -10,7 +10,7 @@
 STEPS = 3
 MESH = pl.DeviceIdType.MESH
 PAD = 8
-ROWS = 16
+ROWS = 32
 CHUNKS = 4
 F32 = jnp.float32
 BF16 = jnp.bfloat16
@@ -29,11 +29,11 @@
 
 
 def kernel(
-    n, shots, prev_hbm, now_hbm, diag_hbm, cross_hbm, green_hbm, delays, past, rec_cell, emit_cell,
+    n, shots, prev_hbm, now_hbm, diag_hbm, cross_hbm, green_hbm, delays, past_hbm, rec_hbm, emit_hbm,
     before_hbm, after_hbm, recorded,
-    ua, ub, diag, cross, green, series, send_edge, recv_edge, send_sum, recv_sum,
+    past, rec_cell, emit_cell, ua, ub, diag, cross, green, series, send_edge, recv_edge, send_sum, recv_sum,
     rec_rows, rec_lanes, emit_rows, emit_lanes, weights,
-    now_sem, prev_sem, coef_sem, green_sem, green_send, green_recv, pass_send, pass_recv,
+    small_sem, now_sem, prev_sem, coef_sem, green_sem, green_send, green_recv, pass_send, pass_recv,
     edge_send, edge_recv, sum_send, sum_recv, out_sem,
 ):
     me = lax.axis_index("brick")
@@ -64,6 +64,14 @@
 
     for x in order:
         now_copy(x).start()
+    small = [
+        pltpu.make_async_copy(source, target, small_sem.at[i])
+        for i, (source, target) in enumerate(
+            ((past_hbm, past), (rec_hbm, rec_cell), (emit_hbm, emit_cell))
+        )
+    ]
+    for copy in small:
+        copy.start()
 
     barrier = pltpu.get_barrier_semaphore()
     for i in range(1, n):
@@ -171,6 +179,8 @@
     for k in range(CHUNKS):
         send_edges(ub, 0, k)
 
+    for copy in small:
+        copy.wait()
     cells = rec_cell[...]
     row_col = column_of((cells // nz).astype(F32))
     lane_col = column_of((cells % nz).astype(F32))
@@ -187,7 +197,7 @@
     emit_rows[:, pl.ds(points, points)] = hits
     emit_lanes[...] = jnp.where(lanes == column_of((cells % nz).astype(F32)), 1.0, 0.0)
     series[...] = jnp.zeros(series.shape, F32)
-    series[pl.ds(0, hist), :] = past[...]
+    series[pl.ds(0, hist), :] = past[...].astype(F32).reshape(hist, points)
 
     def record(field, t):
         picked = jnp.zeros((points, nz), F32)
@@ -252,9 +262,9 @@
         weights[pl.ds(0, points), :] = upper
         weights[pl.ds(points, points), :] = (spread - upper.astype(F32)).astype(BF16)
 
-    def add_emission(field, x, start, rows):
-        field[1 + x, pl.ds(PAD + start, rows)] += jnp.dot(
-            emit_rows[pl.ds(x * ny + start, rows), :], weights[...], preferred_element_type=F32
+    def emission_on(x):
+        return jnp.dot(
+            emit_rows[pl.ds(x * ny, ny), :], weights[...], preferred_element_type=F32
         )
 
     lane = lax.broadcasted_iota(jnp.int32, (ROWS, nz), 1)
@@ -298,7 +308,7 @@
             earlier[1 + x, here] = twice - earlier[1 + x, here] + second + 0.5 * mixed
             return 0
 
-        lax.fori_loop(0, rows // ROWS, body, 0)
+        lax.fori_loop(0, rows // ROWS, body, 0, unroll=2)
 
     for x in range(1, cx - 1):
         now_copy(x).wait()
@@ -329,14 +339,15 @@
                 cross_copy(x).wait()
         emit_finish(t)
         for x in range(1, cx - 1):
-            add_emission(earlier, x, 0, ny)
+            earlier[1 + x, inner] += emission_on(x)
+        for x in (0, cx - 1):
+            earlier[1 + x, inner] -= emission_on(x)
         take_edges(current, t, 0)
         for k in range(CHUNKS):
             if k + 1 < CHUNKS:
                 take_edges(current, t, k + 1)
             for x in (0, cx - 1):
                 advance(earlier, current, x, k * chunk, chunk)
-                add_emission(earlier, x, k * chunk, chunk)
             if t + 1 < STEPS:
                 send_edges(earlier, t + 1, k)
         if t == STEPS - 2:
@@ -386,9 +397,12 @@
             jax.ShapeDtypeStruct(field_prev.shape, F32),
             jax.ShapeDtypeStruct((STEPS, points), F32),
         ),
-        in_specs=[hbm] * 5 + [pl.BlockSpec(memory_space=pltpu.SMEM)] + [vmem] * 3,
+        in_specs=[hbm] * 5 + [pl.BlockSpec(memory_space=pltpu.SMEM)] + [hbm] * 3,
         out_specs=(hbm, hbm, vmem),
         scratch_shapes=[
+            pltpu.VMEM(past.shape, BF16),
+            pltpu.VMEM(rec_cell.shape, jnp.int32),
+            pltpu.VMEM(emit_cell.shape, jnp.int32),
             pltpu.VMEM((cx + 2, ny + 2 * PAD, nz), F32),
             pltpu.VMEM((cx + 2, ny + 2 * PAD, nz), F32),
             pltpu.VMEM((3, cx, ny, nz), F32),
@@ -404,6 +418,7 @@
             pltpu.VMEM((cx * ny, 2 * points), BF16),
             pltpu.VMEM((points, nz), F32),
             pltpu.VMEM((2 * points, nz), BF16),
+            dma((3,)),
             dma((cx,)),
             dma((cx,)),
             dma((2, cx)),
@@ -419,7 +434,7 @@
             dma((2,)),
         ],
         compiler_params=pltpu.CompilerParams(
-            collective_id=0, has_side_effects=True, vmem_limit_bytes=48 * 1024 * 1024
+            collective_id=0, has_side_effects=True, vmem_limit_bytes=62 * 1024 * 1024
         ),
     )(
         field_prev,
@@ -428,7 +443,7 @@
         cross_coef,
         green,
         delays,
-        past.reshape(hist, points).astype(F32),
+        past,
         rec_cell,
         emit_cell,
     )

time: 53.5 us -> 46.7 us (0.87)
  Pallas kernels: 44 us -> 38.7 us
  local copies, waits for them, and re-layouts: 7.3 us -> 5.85 us
    pallas_call x1, Pallas kernels: 44 us -> 38.7 us  [on_device(): pl.pallas_call(functools.partial(kernel, n, shots), out_shape=(jax.ShapeD...]
    unnamed x14 -> x3, local copies, waits for them, and re-layouts: 7.3 us -> 5.85 us
    convert_element_type x1 -> x0, other arithmetic: 0.68 us -> none  [on_device(): past.reshape(hist, points).astype(F32)]
    reshape x1, other arithmetic: 0.56 us -> 1.23 us  [on_device(): return (before, after, recorded.astype(BF16).reshape(STEPS, 1, points))]
where the time goes in v2:
time: 46.7 us; the launch traced here: 46.5 us
  Pallas kernels  38.7 us (83%)
  local copies, waits for them, and re-layouts  5.85 us (13%)
  other arithmetic  1.23 us (3%)
  between operations  0.64 us (1%)
    pallas_call x1, Pallas kernels, on_device(): pl.pallas_call(functools.partial(kernel, n, shots), out_shape=(jax.ShapeD...  38.7 us
    unnamed x3, local copies, waits for them, and re-layouts  5.85 us
    reshape x1, other arithmetic, on_device(): return (before, after, recorded.astype(BF16).reshape(STEPS, 1, points))  1.23 us

profile of v2, /device:TPU:0, one launch (start us, length us, event | category | flops | bytes accessed | tf_op | source)
XLA Modules:
  0.0 46.5 jit_solution(15389247686032121650)
XLA Ops:
  0.6 1.3 %copy.12.past_hbm = bf16[8,1,128]{2,1,0:T(2,128)(2,1)} copy(bf16[8,1,128]{2,0,1:T(8,128)(2,1)} %param.15) | data formatting | bytes 4096 | tf_op args[6]
  1.9 38.7 %shard_map.112 = (f32[1,4,256,256]{3,2,1,0:T(8,128)}, f32[1,4,256,256]{3,2,1,0:T(8,128)}, f32[3,128]{1,0:T(4,128)}) custom-call(f32[1,4,256,256]{3,2,1,0:T(8,128)} %prev_hbm.1, f32[1,4,256,256]{3,2,1,0:T(8,128)} %now_hbm.1, f32[3,4,256,256]{3,2,1,0:T(8,128)} %diag_hbm.1, f32[3,4,256,256]{3,2,1,0:T(8,128)} %cross_hbm.1, bf16[1,1024,128]{2,1,0:T(8,128)(2,1)} %green_hbm.1, ...), custom_call_target="tpu_custom_call" | custom-call | tf_op jit(solution)/shard_map/pallas_call | solution.py:393
  40.7 1.2 %convert_bitcast_fusion = bf16[3,1,128]{2,0,1:T(4,128)(2,1)} fusion(f32[3,128]{1,0:T(4,128)} %get-tuple-element.8), kind=kLoop, calls=%fused_computation | loop fusion | flops 384 | bytes 2304 | tf_op jit(solution)/shard_map/reshape | solution.py:450
  41.9 2.3 %copy.15 = f32[1,4,256,256]{3,2,1,0:T(8,128)} copy(f32[1,4,256,256]{3,2,1,0:T(8,128)} %get-tuple-element.12) | data formatting | bytes 2097152
  44.2 2.3 %copy.16 = f32[1,4,256,256]{3,2,1,0:T(8,128)} copy(f32[1,4,256,256]{3,2,1,0:T(8,128)} %get-tuple-element.13) | data formatting | bytes 2097152

commit v3 on v2

--- a/solution.py
+++ b/solution.py
@@ -152,15 +152,12 @@
     def hears_from(side):
         return me > 0 if side == 0 else me < n - 1
 
-    def send_edges(field, t, k):
-        for side in (0, 1):
-            plane = cx if side == 0 else 1
-            send_edge[t, side, pl.ds(k * chunk, chunk)] = field[
-                plane, pl.ds(PAD + k * chunk, chunk)
-            ].astype(BF16)
-
-            @pl.when(sends_to(side))
-            def _():
+    def send_edges(field, t, side):
+        send_edge[t, side] = field[cx if side == 0 else 1, inner].astype(BF16)
+
+        @pl.when(sends_to(side))
+        def _():
+            for k in range(CHUNKS):
                 edge_copy(t, side, k).start()
 
     def take_edges(field, t, k):
@@ -175,9 +172,9 @@
                 ].astype(F32)
 
     now_copy(0).wait()
+    send_edges(ub, 0, 1)
     now_copy(cx - 1).wait()
-    for k in range(CHUNKS):
-        send_edges(ub, 0, k)
+    send_edges(ub, 0, 0)
 
     for copy in small:
         copy.wait()
@@ -197,7 +194,7 @@
     emit_rows[:, pl.ds(points, points)] = hits
     emit_lanes[...] = jnp.where(lanes == column_of((cells % nz).astype(F32)), 1.0, 0.0)
     series[...] = jnp.zeros(series.shape, F32)
-    series[pl.ds(0, hist), :] = past[...].astype(F32).reshape(hist, points)
+    series[pl.ds(0, hist), :] = past[...]
 
     def record(field, t):
         picked = jnp.zeros((points, nz), F32)
@@ -328,28 +325,29 @@
             for i in range(1, half):
                 green_wait(i)
                 pass_copy(i, core).start()
-            own_green.wait()
-            green_wait(0)
-            for i in range(1, half):
-                pass_copy(i, 1 - core).wait_recv()
-            emit_start(t)
             for x in (0, cx - 1):
                 prev_copy(x).wait()
                 diag_copy(x).wait()
                 cross_copy(x).wait()
-        emit_finish(t)
-        for x in range(1, cx - 1):
-            earlier[1 + x, inner] += emission_on(x)
-        for x in (0, cx - 1):
-            earlier[1 + x, inner] -= emission_on(x)
         take_edges(current, t, 0)
         for k in range(CHUNKS):
             if k + 1 < CHUNKS:
                 take_edges(current, t, k + 1)
             for x in (0, cx - 1):
                 advance(earlier, current, x, k * chunk, chunk)
+        if t == 0:
+            own_green.wait()
+            green_wait(0)
+            for i in range(1, half):
+                pass_copy(i, 1 - core).wait_recv()
+            emit_start(t)
+        emit_finish(t)
+        for side, x in ((0, cx - 1), (1, 0)):
+            earlier[1 + x, inner] += emission_on(x)
             if t + 1 < STEPS:
-                send_edges(earlier, t + 1, k)
+                send_edges(earlier, t + 1, side)
+        for x in range(1, cx - 1):
+            earlier[1 + x, inner] += emission_on(x)
         if t == STEPS - 2:
             before = pltpu.make_async_copy(
                 earlier.at[pl.ds(1, cx), inner], before_hbm.at[0], out_sem.at[0]
@@ -388,6 +386,7 @@
     half = shots // 2
     vmem = pl.BlockSpec(memory_space=pltpu.VMEM)
     hbm = pl.BlockSpec(memory_space=pl.ANY)
+    fixed = pl.BlockSpec(memory_space=pltpu.HBM)
     dma = pltpu.SemaphoreType.DMA
     depth = -(-(hist + STEPS) // 8) * 8
     before, after, recorded = pl.pallas_call(
@@ -397,10 +396,10 @@
             jax.ShapeDtypeStruct(field_prev.shape, F32),
             jax.ShapeDtypeStruct((STEPS, points), F32),
         ),
-        in_specs=[hbm] * 5 + [pl.BlockSpec(memory_space=pltpu.SMEM)] + [hbm] * 3,
+        in_specs=[fixed] * 5 + [pl.BlockSpec(memory_space=pltpu.SMEM)] + [fixed] * 3,
         out_specs=(hbm, hbm, vmem),
         scratch_shapes=[
-            pltpu.VMEM(past.shape, BF16),
+            pltpu.VMEM((hist, points), F32),
             pltpu.VMEM(rec_cell.shape, jnp.int32),
             pltpu.VMEM(emit_cell.shape, jnp.int32),
             pltpu.VMEM((cx + 2, ny + 2 * PAD, nz), F32),
@@ -434,7 +433,7 @@
             dma((2,)),
         ],
         compiler_params=pltpu.CompilerParams(
-            collective_id=0, has_side_effects=True, vmem_limit_bytes=62 * 1024 * 1024
+            collective_id=0, has_side_effects=True, vmem_limit_bytes=48 * 1024 * 1024
         ),
     )(
         field_prev,
@@ -443,7 +442,7 @@
         cross_coef,
         green,
         delays,
-        past,
+        past.reshape(hist, points).astype(F32),
         rec_cell,
         emit_cell,
     )

time: 46.7 us -> 45.1 us (0.966)
  Pallas kernels: 38.7 us -> 35.7 us
  local copies, waits for them, and re-layouts: 5.85 us -> 7.3 us
    pallas_call x1, Pallas kernels: 38.7 us -> 35.7 us  [on_device(): pl.pallas_call(functools.partial(kernel, n, shots), out_shape=(jax.ShapeD...]
    unnamed x3 -> x14, local copies, waits for them, and re-layouts: 5.85 us -> 7.3 us
    convert_element_type x0 -> x1, other arithmetic: none -> 0.68 us  [on_device(): past.reshape(hist, points).astype(F32)]
    reshape x1, other arithmetic: 1.23 us -> 0.56 us  [on_device(): return (before, after, recorded.astype(BF16).reshape(STEPS, 1, points))]
where the time goes in v3:
time: 45.1 us; the launch traced here: 44.9 us
  Pallas kernels  35.7 us (79%)
  local copies, waits for them, and re-layouts  7.3 us (16%)
  other arithmetic  1.25 us (3%)
  between operations  0.65 us (1%)
    pallas_call x1, Pallas kernels, on_device(): pl.pallas_call(functools.partial(kernel, n, shots), out_shape=(jax.ShapeD...  35.7 us
    unnamed x14, local copies, waits for them, and re-layouts  7.3 us

profile of v3, /device:TPU:0, one launch (start us, length us, event | category | flops | bytes accessed | tf_op | source)
XLA Modules:
  0.0 44.9 jit_solution(16421055146675606942)
XLA Ops:
  0.6 0.7 %bitcast_convert_fusion.past_hbm = f32[8,128]{1,0:T(8,128)S(1)} fusion(bf16[8,1,128]{2,0,1:T(8,128)(2,1)} %param.15), kind=kLoop, calls=%fused_computation | loop fusion | flops 1024 | bytes 6144 | tf_op jit(solution)/shard_map/convert_element_type | solution.py:445
  1.3 0.0 copy-start
  1.3 1.2 %copy-done = f32[1,4,256,256]{3,2,1,0:T(8,128)S(1)} copy-done((f32[1,4,256,256]{3,2,1,0:T(8,128)S(1)}, f32[1,4,256,256]{3,2,1,0:T(8,128)}, u32[]{:S(2)}) %copy-start) | copy-done | bytes 1048600
  2.5 0.0 copy-start.1
  2.5 1.2 %copy-done.1 = f32[1,4,256,256]{3,2,1,0:T(8,128)S(1)} copy-done((f32[1,4,256,256]{3,2,1,0:T(8,128)S(1)}, f32[1,4,256,256]{3,2,1,0:T(8,128)}, u32[]{:S(2)}) %copy-start.1) | copy-done | bytes 1048600
  3.8 0.0 copy-start.2
  3.8 0.9 %copy-done.2 = bf16[1,1024,128]{2,1,0:T(8,128)(2,1)S(1)} copy-done((bf16[1,1024,128]{2,1,0:T(8,128)(2,1)S(1)}, bf16[1,1024,128]{2,1,0:T(8,128)(2,1)}, u32[]{:S(2)}) %copy-start.2) | copy-done | bytes 262168
  4.7 0.0 copy-start.3
  4.7 0.7 %copy-done.3 = s32[4]{0:T(128)S(1)} copy-done((s32[4]{0:T(128)S(1)}, s32[4]{0:T(128)}, u32[]{:S(2)}) %copy-start.3) | copy-done | bytes 40
  5.4 0.0 copy-start.4
  5.4 0.7 %copy-done.4 = s32[1,128]{1,0:T(1,128)S(1)} copy-done((s32[1,128]{1,0:T(1,128)S(1)}, s32[1,128]{1,0:T(1,128)}, u32[]{:S(2)}) %copy-start.4) | copy-done | bytes 536
  6.0 0.0 copy-start.5
  6.0 0.7 %copy-done.5 = s32[1,128]{1,0:T(1,128)S(1)} copy-done((s32[1,128]{1,0:T(1,128)S(1)}, s32[1,128]{1,0:T(1,128)}, u32[]{:S(2)}) %copy-start.5) | copy-done | bytes 536
  6.7 35.7 %shard_map.112 = (f32[1,4,256,256]{3,2,1,0:T(8,128)S(1)}, f32[1,4,256,256]{3,2,1,0:T(8,128)S(1)}, f32[3,128]{1,0:T(4,128)S(1)}) custom-call(f32[1,4,256,256]{3,2,1,0:T(8,128)S(1)} %copy-done, f32[1,4,256,256]{3,2,1,0:T(8,128)S(1)} %copy-done.1, f32[3,4,256,256]{3,2,1,0:T(8,128)} %diag_hbm.1, f32[3,4,256,256]{3,2,1,0:T(8,128)} %cross_hbm.1, ...), custom_call_target="tpu_custom_call" | custom-call | tf_op jit(solution)/shard_map/pallas_call | solution.py:392
  42.4 0.6 %convert_bitcast_fusion = bf16[3,1,128]{2,0,1:T(4,128)(2,1)} fusion(f32[3,128]{1,0:T(4,128)S(1)} %get-tuple-element.8), kind=kLoop, calls=%fused_computation.1 | loop fusion | flops 384 | bytes 2304 | tf_op jit(solution)/shard_map/reshape | solution.py:449
  42.9 1.0 %copy.14 = f32[1,4,256,256]{3,2,1,0:T(8,128)} copy(f32[1,4,256,256]{3,2,1,0:T(8,128)S(1)} %get-tuple-element.12) | data formatting | bytes 2097152
  43.9 1.0 %copy.15 = f32[1,4,256,256]{3,2,1,0:T(8,128)} copy(f32[1,4,256,256]{3,2,1,0:T(8,128)S(1)} %get-tuple-element.13) | data formatting | bytes 2097152
Async XLA Ops:
  1.3 1.2 %copy-start = (f32[1,4,256,256]{3,2,1,0:T(8,128)S(1)}, f32[1,4,256,256]{3,2,1,0:T(8,128)}, u32[]{:S(2)}) copy-start(f32[1,4,256,256]{3,2,1,0:T(8,128)} %prev_hbm.1) | copy-start | bytes 3145732
  2.5 1.2 %copy-start.1 = (f32[1,4,256,256]{3,2,1,0:T(8,128)S(1)}, f32[1,4,256,256]{3,2,1,0:T(8,128)}, u32[]{:S(2)}) copy-start(f32[1,4,256,256]{3,2,1,0:T(8,128)} %now_hbm.1) | copy-start | bytes 3145732
  3.8 0.9 %copy-start.2 = (bf16[1,1024,128]{2,1,0:T(8,128)(2,1)S(1)}, bf16[1,1024,128]{2,1,0:T(8,128)(2,1)}, u32[]{:S(2)}) copy-start(bf16[1,1024,128]{2,1,0:T(8,128)(2,1)} %green_hbm.1) | copy-start | bytes 786436
  4.7 0.7 %copy-start.3 = (s32[4]{0:T(128)S(1)}, s32[4]{0:T(128)}, u32[]{:S(2)}) copy-start(s32[4]{0:T(128)} %delays.1) | copy-start | bytes 52
  5.4 0.7 %copy-start.4 = (s32[1,128]{1,0:T(1,128)S(1)}, s32[1,128]{1,0:T(1,128)}, u32[]{:S(2)}) copy-start(s32[1,128]{1,0:T(1,128)} %rec_hbm.1) | copy-start | bytes 1540
  6.0 0.7 %copy-start.5 = (s32[1,128]{1,0:T(1,128)S(1)}, s32[1,128]{1,0:T(1,128)}, u32[]{:S(2)}) copy-start(s32[1,128]{1,0:T(1,128)} %emit_hbm.1) | copy-start | bytes 1540
